TPU v7x, 256 devices: a whole 4x4x8 slice. The times are simulated.
256 devices in a mesh: dom: 64 (over x, y_hi, z), pot: 4 (over y_lo, core).
Axes of the slice: x: 4, y: 4 (y_hi: 2, y_lo: 2; y = y_hi * 2 + y_lo), z: 8, core: 2. Of those that a mesh axis runs over, the one named last changes fastest.
Arguments:
- band_orbitals: float32 [4, 128, 192, 128], P(None, 'dom'), may hold values from -7 to 11, as said below
- local_potential: float32 [128, 192, 128], P('dom'), may hold values from 0.2 to 2
- band_shift: float32 [4], replicated, may hold values from 0.1 to 1
- trial_potentials: float32 [8, 128, 192, 128], P('pot', 'dom'), may hold values from -0.5 to 2
- projector_blocks: float32 [8, 2, 192, 128], replicated, may hold values from 0.2 to 1.8
- atom_plane: int32 [8], replicated, may hold values from 0 to 126, as said below
- projector_weight: float32 [8], replicated, may hold values from 0.5 to 4
Outputs:
- solution: float32 [8, 4, 128, 192, 128], P('pot', None, 'dom')
- response: float32 [8, 8], P('pot')
Inputs may be any that keep to these rules, and one draw needn't show every extreme that they name: `band_orbitals`: orbitals of the nanocrystal's occupied bands. The block of atom a covers planes atom_plane[a] to atom_plane[a] + 1.
All inputs are finite; a program needn't handle non-finite values.
Results may differ from a plain program's by a relative error of at most 0.0003.
Values sent between devices are 32-bit elements; how exact they have to be, the bound alone decides.
A program may use at most 128 MiB of HBM per device.

v0:
```python
import jax
import jax.numpy as jnp
from jax import lax
from jax.sharding import PartitionSpec as P

ITERS = 2


NEAR_COEF = 4.0 / 3.0
FAR_COEF = -1.0 / 12.0
SELF_COEF = -2.5
HIGHEST = lax.Precision.HIGHEST


def padded(x, sides, width):
    for axis, dim in sides:
        count, length = (lax.axis_size(axis), x.shape[dim])
        up = [(i, (i + 1) % count) for i in range(count)]
        down = [(j, i) for i, j in up]
        last = lax.slice_in_dim(x, length - width, length, axis=dim)
        initial = lax.slice_in_dim(x, 0, width, axis=dim)
        before = lax.ppermute(last, axis, up)
        after = lax.ppermute(initial, axis, down)
        x = jnp.concatenate([before, x, after], axis=dim)
    return x


def kinetic_from(extended):
    center = extended[:, :, 2:-2]
    total = 3.0 * SELF_COEF * center
    total = (
        total
        + FAR_COEF * (extended[:, :, :-4] + extended[:, :, 4:])
        + NEAR_COEF * (extended[:, :, 1:-3] + extended[:, :, 3:-1])
    )
    for axis_num in (3, 4):
        total = (
            total
            + FAR_COEF * (jnp.roll(center, 2, axis_num) + jnp.roll(center, -2, axis_num))
            + NEAR_COEF * (jnp.roll(center, 1, axis_num) + jnp.roll(center, -1, axis_num))
        )
    return -0.5 * total


def global_sum(values):
    return lax.psum(values, "dom")


def shards(
    band_orbitals,
    local_potential,
    band_shift,
    trial_potentials,
    projector_blocks,
    atom_plane,
    projector_weight,
):
    band_count, width_x, grid_y, grid_z = band_orbitals.shape
    cell_count = width_x * lax.axis_size("dom") * grid_y * grid_z
    span_len = projector_blocks.shape[1]
    block_cells = span_len * grid_y * grid_z
    anchor = lax.axis_index("dom") * width_x
    planes = atom_plane[:, None, None] + lax.broadcasted_iota(jnp.int32, (1, span_len, 1), 1)
    places = anchor + lax.broadcasted_iota(jnp.int32, (1, 1, width_x), 2)
    selector = (planes == places).astype(jnp.float32)
    projectors = jnp.einsum("awc,awyz->acyz", selector, projector_blocks, precision=HIGHEST)
    diag_shift = local_potential[None, None] + band_shift[None, :, None, None, None]
    source = -trial_potentials[:, None] * band_orbitals[None]
    solution = jnp.zeros_like(source)
    residual = source
    direction = source
    norm_now = global_sum(jnp.sum(source * source, axis=(2, 3, 4))) / cell_count
    for sweep in range(ITERS):
        extended = padded(direction, (("dom", 2),), 2)
        local_term = kinetic_from(extended) + diag_shift * direction
        proj_part = jnp.einsum("pnxyz,axyz->pna", direction, projectors, precision=HIGHEST)
        band_part = jnp.einsum("pnxyz,mxyz->pnm", direction, band_orbitals, precision=HIGHEST)
        proj_sum, band_sum = lax.psum((proj_part, band_part), "dom")
        proj_over = proj_sum / block_cells
        band_over = band_sum / cell_count
        op_image = (
            local_term
            + jnp.einsum(
                "pna,axyz->pnxyz", projector_weight * proj_over, projectors, precision=HIGHEST
            )
            + jnp.einsum("pnm,mxyz->pnxyz", band_over, band_orbitals, precision=HIGHEST)
        )
        curvature = lax.psum(jnp.sum(direction * op_image, axis=(2, 3, 4)), "dom") / cell_count
        step_len = (norm_now / curvature)[:, :, None, None, None]
        solution = solution + step_len * direction
        if sweep + 1 < ITERS:
            residual = residual - step_len * op_image
            norm_next = global_sum(jnp.sum(residual * residual, axis=(2, 3, 4))) / cell_count
            direction = residual + (norm_next / norm_now)[:, :, None, None, None] * direction
            norm_now = norm_next
    density = 2.0 * jnp.sum(band_orbitals[None] * solution, axis=1)
    values = jnp.einsum(
        "pxyz,qxyz->pq",
        density,
        lax.all_gather(trial_potentials, "pot", axis=0, tiled=True),
        precision=HIGHEST,
    )
    response = lax.psum(values, "dom") / cell_count
    return (solution, response)


def solution(mesh):
    placed = (
        P(None, "dom", None, None),
        P("dom", None, None),
        P(),
        P("pot", "dom", None, None),
        P(),
        P(),
        P(),
    )
    return jax.shard_map(
        shards,
        mesh=mesh,
        in_specs=placed,
        out_specs=(P("pot", None, "dom", None, None), P("pot", None)),
        check_vma=False,
    )
```

profile of v0, /device:TPU:8, one launch (start us, length us, event | category | flops | bytes accessed | tf_op | source)
XLA Modules:
  0.0 1235.7 jit_solution(2164677142424889418)
XLA Ops:
  11.8 8.0 collective-permute-start.1
  19.9 2.2 fusion.107
  24.9 3.6 fusion.44
  28.5 9.0 fusion.56
  37.5 8.6 fusion.53
  46.2 184.2 %all-reduce.2 = (f32[2,4,8]{2,1,0:T(4,128)S(1)}, f32[2,4,4]{2,1,0:T(4,128)}) all-reduce(f32[2,4,8]{2,1,0:T(4,128)S(1)} %fusion.56, f32[2,4,4]{2,1,0:T(4,128)S(1)} %fusion.53), channel_id=1, replica_groups=mesh['dom'=64,'pot'=4] {'dom'}, use_global_device_ids=true, to_apply=%region_2.3 | all-reduce | flops 96 | bytes 768 | tf_op jit(solution)/shard_map/psum | solution.py:78
  230.4 4.2 fusion.40
  237.7 2.6 fusion.106
  240.3 14.2 %fusion.4 = (f32[2,4]{1,0:T(2,128)S(1)}, f32[2,4]{1,0:T(2,128)S(1)}, f32[2,4,2,192,128]{4,1,3,2,0:T(4,128)}) fusion(f32[4,2,192,128]{3,0,2,1:T(4,128)S(1)} %copy-done.3, f32[2,2,192,128]{3,2,1,0:T(8,128)S(1)} %neg.4, f32[2,4,4]{2,1,0:T(4,128)S(1)} %copy-done.25, f32[2,4,2,192,128]{4,1,3,2,0:T(4,128)S(1)} %fusion.40, ...), kind=kOutput, calls=%fused_computation.11 | convolution fusion | flops 34209808 | bytes 22413504 | tf_op jit(solution)/shard_map/pnm,mxyz->pnxyz/dot_general | solution.py:86
  254.5 176.4 %all-reduce.1 = (f32[2,4]{1,0:T(2,128)S(1)}, f32[2,4]{1,0:T(2,128)S(1)}) all-reduce(f32[2,4]{1,0:T(2,128)S(1)} %get-tuple-element.7, f32[2,4]{1,0:T(2,128)S(1)} %get-tuple-element.6), channel_id=1, replica_groups=mesh['dom'=64,'pot'=4] {'dom'}, use_global_device_ids=true, to_apply=%region_5.6 | all-reduce | flops 16 | bytes 128 | tf_op jit(solution)/shard_map/psum | solution.py:88
  430.9 2.5 multiply_reduce_fusion.2
  433.3 179.3 %psum.67 = f32[2,4]{1,0:T(2,128)S(1)} all-reduce(f32[2,4]{1,0:T(2,128)S(1)} %multiply_reduce_fusion.2), channel_id=1, replica_groups=mesh['dom'=64,'pot'=4] {'dom'}, use_global_device_ids=true, to_apply=%region_7.8 | all-reduce | flops 8 | bytes 64 | tf_op jit(solution)/shard_map/psum | solution.py:46
  612.7 2.2 fusion.15
  614.9 2.6 fusion.99
  621.6 8.5 convolution_bitcast_fusion
  630.1 8.5 fusion.50
  638.7 7.8 collective-permute-start.3
  647.2 194.1 %all-reduce = (f32[2,4,8]{2,1,0:T(4,128)}, f32[2,4,4]{2,1,0:T(4,128)}) all-reduce(f32[2,4,8]{2,1,0:T(4,128)S(1)} %fusion.50, f32[2,4,4]{2,1,0:T(4,128)S(1)} %convolution_bitcast_fusion), channel_id=1, replica_groups=mesh['dom'=64,'pot'=4] {'dom'}, use_global_device_ids=true, to_apply=%region_8.9 | all-reduce | flops 96 | bytes 768 | tf_op jit(solution)/shard_map/psum | solution.py:78
  841.2 4.2 fusion.38
  850.1 12.3 multiply_reduce_fusion.1
  862.3 176.6 %psum.70 = f32[2,4]{1,0:T(2,128)S(1)} all-reduce(f32[2,4]{1,0:T(2,128)S(1)} %multiply_reduce_fusion.1), channel_id=1, replica_groups=mesh['dom'=64,'pot'=4] {'dom'}, use_global_device_ids=true, to_apply=%region_11.12 | all-reduce | flops 8 | bytes 64 | tf_op jit(solution)/shard_map/psum | solution.py:88
  1039.0 3.6 multiply_reduce_fusion
  1043.9 5.7 fusion.61
  1049.7 178.4 %psum.71 = f32[2,8]{1,0:T(2,128)S(1)} all-reduce(f32[2,8]{1,0:T(2,128)S(1)} %fusion.61), channel_id=1, replica_groups=mesh['dom'=64,'pot'=4] {'dom'}, use_global_device_ids=true, to_apply=%region_13.14 | all-reduce | flops 16 | bytes 128 | tf_op jit(solution)/shard_map/psum | solution.py:103
  (91 shorter events, 21.7 us)
Async XLA Ops:
  7.2 17.7 %copy-start = (f32[8,2,192,128]{3,2,1,0:T(8,128)S(1)}, f32[8,2,192,128]{3,2,1,0:T(8,128)}, u32[]{:S(2)}) copy-start(f32[8,2,192,128]{3,2,1,0:T(8,128)} %param.11) | copy-start | bytes 4718596
  7.2 1036.7 %all-gather.2.cloned.1.call-start = ((), (), s32[]{:S(2)}) async-start(), calls=%async_computation | async-start | bytes 1966080 | tf_op jit(solution)/shard_map/all_gather | solution.py:100
  9.9 230.3 %collective-permute-start = (f32[2,4,2,192,128]{4,1,3,2,0:T(4,128)S(1)}, f32[2,4,2,192,128]{4,1,3,2,0:T(4,128)}, u32[]{:S(2)}, u32[]{:S(2)}) collective-permute-start(f32[2,4,2,192,128]{4,1,3,2,0:T(4,128)S(1)} %broadcast_multiply_fusion), channel_id=1, source_target_pairs={{0,4},{4,8},{8,12},{12,16},{16,20},{20,24},{24,28},{28,32},{32,36}... | collective-permute-start | bytes 4718600 | tf_op jit(solution)/shard_map/ppermute | solution.py:22
  11.8 228.4 %collective-permute-start.1 = (f32[2,4,2,192,128]{4,1,3,2,0:T(4,128)S(1)}, f32[2,4,2,192,128]{4,1,3,2,0:T(4,128)}, u32[]{:S(2)}, u32[]{:S(2)}) collective-permute-start(f32[2,4,2,192,128]{4,1,3,2,0:T(4,128)S(1)} %broadcast_multiply_fusion), channel_id=1, source_target_pairs={{4,0},{8,4},{12,8},{16,12},{20,16},{24,20},{28,24},{32,28},{36,32}... | collective-permute-start | bytes 4718600 | tf_op jit(solution)/shard_map/ppermute | solution.py:23
  22.0 2.7 copy-start.24
  24.8 3.6 copy-start.2
  28.5 9.0 copy-start.4
  28.5 9.0 copy-start.6
  37.5 8.7 copy-start.27
  46.1 188.5 %copy-start.22 = (f32[8]{0:T(128)}, f32[8]{0:T(128)S(1)}, u32[]{:S(2)}) copy-start(f32[8]{0:T(128)S(1)} %broadcast_multiply_fusion.3) | copy-start | bytes 100
  230.4 4.3 copy-start.15
  230.4 4.3 copy-start.23
  234.9 5.4 copy-start.13
  237.6 2.6 copy-start.3
  237.6 2.6 copy-start.16
  237.7 2.6 copy-start.17
  621.6 8.5 copy-start.5
  638.6 209.7 %collective-permute-start.2 = (f32[2,4,2,192,128]{4,1,3,2,0:T(4,128)S(1)}, f32[2,4,2,192,128]{4,1,3,2,0:T(4,128)}, u32[]{:S(2)}, u32[]{:S(2)}) collective-permute-start(f32[2,4,2,192,128]{4,1,3,2,0:T(4,128)S(1)} %fusion.15), channel_id=1, source_target_pairs={{0,4},{4,8},{8,12},{12,16},{16,20},{20,24},{24,28},{28,32},{32,36}... | collective-permute-start | bytes 4718600 | tf_op jit(solution)/shard_map/ppermute | solution.py:22
  638.7 209.6 %collective-permute-start.3 = (f32[2,4,2,192,128]{4,1,3,2,0:T(4,128)S(1)}, f32[2,4,2,192,128]{4,1,3,2,0:T(4,128)}, u32[]{:S(2)}, u32[]{:S(2)}) collective-permute-start(f32[2,4,2,192,128]{4,1,3,2,0:T(4,128)S(1)} %fusion.15), channel_id=1, source_target_pairs={{4,0},{8,4},{12,8},{16,12},{20,16},{24,20},{28,24},{32,28},{36,32}... | collective-permute-start | bytes 4718600 | tf_op jit(solution)/shard_map/ppermute | solution.py:23
  847.3 2.7 copy-start.14
  847.3 2.7 copy-start.18
  847.3 2.7 copy-start.19
  847.3 2.7 copy-start.26
  850.1 188.9 %copy-start.21 = (f32[2,4]{1,0:T(2,128)S(1)}, f32[2,4]{1,0:T(2,128)}, u32[]{:S(2)}) copy-start(f32[2,4]{1,0:T(2,128)} %copy-done.20) | copy-start | bytes 100
  (9 other events, 17.0 us)
Sparse Core Ops, SparseCore 0:
  433.5 19.6 all-gather.1
where the time goes:
time: 1240 us
  blocking collectives  1090 us (88%)
  matrix products  78.9 us (6%)
  local copies, waits for them, and re-layouts  25.6 us (2%)
  starting transfers between devices  17.9 us (1%)
  between operations  14.7 us (1%)
    psum x2, blocking collectives, shards(): proj_sum, band_sum = lax.psum((proj_part, band_part), 'dom')  378 us
    psum x2, blocking collectives, shards(): lax.psum(jnp.sum(direction * op_image, axis=(2, 3, 4)), 'dom') / cell_count  353 us
    psum x1, blocking collectives, global_sum(): return lax.psum(values, 'dom')  179 us
    psum x1, blocking collectives, shards(): response = lax.psum(values, 'dom') / cell_count  178 us
    dot_general x2, matrix products, shards(): jnp.einsum('pnm,mxyz->pnxyz', band_over, band_orbitals, precision=HIGHEST)  26.4 us
  transfers between devices with their start and end apart: 5, of which 0 were waited for; matrix products, arithmetic and copies ran while one was open for 7% of the time, Pallas kernels for 0%

commit v1 on v0

v1 whole, which is shorter than its diff:
```python
import jax
import jax.numpy as jnp
from jax import lax
from jax.experimental import pallas as pl
from jax.experimental.pallas import tpu as pltpu
from jax.sharding import PartitionSpec as P

MESH = pl.DeviceIdType.MESH
F32 = jnp.float32
DOMS, POTS_AXIS = 64, 4
NB, ATOMS, LOC = 4, 8, 2
PAIRS = LOC * NB
NY, NZ, HALF = 192, 128, 96
BLK = 24
KU = ATOMS + NB
CELLS = 128 * 192 * 128
BLOCK_CELLS = 2 * 192 * 128
C1P, C1V, C2P, C2V, C3P, C3V = 0, 2, 4, 6, 8, 10
BCAST = 12
VG = BCAST + 18
ROWS = VG + 3
NSEM = ROWS + 3


def kernel(
    psi_h, lp_h, v_h, proj_h, shift_s, plane_s, weight_s,
    sol_h, resp_o,
    psi, v, lp, proj, vall, stg, ph1, ph2, ph3, vh1, vh2, vh3,
    bb, yb, pj, sol, acc, ct, rowb, slots, lsem, ss, rs, gate,
):
    dom, pot = lax.axis_index("dom"), lax.axis_index("pot")
    right, left = (dom + 1) % DOMS, (dom + DOMS - 1) % DOMS
    mate, part = (pot // 2) * 2 + 1 - pot % 2, (pot + 2) % 4
    plane_xy, zc = dom // 8, dom % 8

    loads = [
        (psi_h.at[pot, :, pl.ds(0, HALF)], stg.at[0, :, pl.ds(0, HALF)]),
        (lp_h.at[:, pl.ds(24 * pot, 24)], stg.at[0, :, pl.ds(HALF, 24)]),
        (psi_h.at[pot, :, pl.ds(HALF, HALF)], stg.at[1, :, pl.ds(0, HALF)]),
        (lp_h.at[:, pl.ds(HALF + 24 * pot, 24)], stg.at[1, :, pl.ds(HALF, 24)]),
        (v_h, v),
        (psi_h, psi),
        (lp_h, lp),
        (proj_h, proj),
    ]
    loads = [pltpu.make_async_copy(a, b, lsem.at[i]) for i, (a, b) in enumerate(loads)]
    for c in loads:
        c.start()

    bar = pltpu.get_barrier_semaphore()

    def greet(d, p):
        pl.semaphore_signal(bar, inc=1, device_id=(d, p), device_id_type=MESH)

    greet(right, pot)
    greet(left, pot)
    greet(dom, mate)
    greet(dom, part)
    for k in range(1, 8):
        greet(plane_xy * 8 + (zc + k) % 8, pot)
        greet(((plane_xy + k) % 8) * 8 + zc, pot)
    for c in loads[:5]:
        c.wait()
    pl.semaphore_wait(bar, 18)

    def remote(i, src, dst, device):
        return pltpu.make_async_remote_copy(
            src, dst, ss.at[i], rs.at[i], device_id=device, device_id_type=MESH
        )

    low, high = pl.ds(0, HALF), pl.ds(HALF, HALF)
    to = ((right, pot), (left, pot))
    near, far = (low, high), (high, low)
    c1p = [remote(C1P + s, stg.at[s], ph1.at[s, pot], to[s]) for s in (0, 1)]
    c1v = [remote(C1V + s, v.at[:, :, near[s]], vh1.at[s], to[s]) for s in (0, 1)]
    c2p = [remote(C2P + s, psi.at[pot, :, far[s]], ph2.at[s, pot], to[s]) for s in (0, 1)]
    c2v = [remote(C2V + s, v.at[:, :, far[s]], vh2.at[s], to[s]) for s in (0, 1)]
    c3p = [remote(C3P + s, ph1.at[s, pot, :, low], ph3.at[s, pot], to[s]) for s in (0, 1)]
    c3v = [remote(C3V + s, vh1.at[s], vh3.at[s], to[s]) for s in (0, 1)]

    def spread(ch, s):
        ref = (ph1, ph2, ph3)[ch]
        i = BCAST + ch * 6 + s * 3
        own, other = ref.at[s, pot], ref.at[s, part]
        return (
            remote(i, own, own, (dom, mate)),
            remote(i + 1, own, own, (dom, part)),
            remote(i + 2, other, other, (dom, mate)),
        )

    spreads = [[spread(ch, s) for s in (0, 1)] for ch in range(3)]
    vown, vpart = vall.at[pl.ds(2 * pot, 2)], vall.at[pl.ds(2 * part, 2)]
    vg = (
        remote(VG, v, vown, (dom, mate)),
        remote(VG + 1, v, vown, (dom, part)),
        remote(VG + 2, vpart, vpart, (dom, mate)),
    )

    def start(copies):
        for c in copies:
            c.start()

    def arrive(copies):
        for c in copies:
            c.wait_recv()

    def pass_on(ch, copies):
        arrive(copies)
        for s in (0, 1):
            spreads[ch][s][1].start()
        for s in (0, 1):
            spreads[ch][s][0].start()

    def pass_mate(ch):
        for s in (0, 1):
            spreads[ch][s][1].wait_recv()
            spreads[ch][s][2].start()

    def gathered(ch):
        for s in (0, 1):
            spreads[ch][s][0].wait_recv()
            spreads[ch][s][2].wait_recv()

    start(c1p)
    start(c1v)
    for k in range(1, 8):
        pl.semaphore_signal(
            gate, inc=1, device_id=(((plane_xy + k) % 8) * 8 + zc, pot), device_id_type=MESH
        )
    loads[5].wait()
    start(c2p)
    start(c2v)

    acc[...] = jnp.zeros_like(acc)
    lane = lax.broadcasted_iota(jnp.int32, (8, NZ), 1)
    wvec = jnp.where((lane >= ATOMS) & (lane < KU), 1.0 / CELLS, 0.0)
    for a in range(ATOMS):
        wvec = jnp.where(lane == a, weight_s[a] / BLOCK_CELLS, wvec)

    def loop(n, body):
        def step(i, _):
            body(i)
            return 0

        lax.fori_loop(0, n, step, 0)

    def rows(j, base=0):
        return pl.multiple_of(base + j * BLK, 8)

    def products(j, base, planes, vref, vrows, pref, prows):
        at = pl.ds(rows(j, base + 8), BLK)
        for w in (0, 1):
            pots = [vref(p, w, pl.ds(rows(j, vrows), BLK)) for p in range(LOC)]
            for n in range(NB):
                orb = pref(n, w, pl.ds(rows(j, prows), BLK))
                for p in range(LOC):
                    bb[p * NB + n, planes + w, at, :] = pots[p] * orb

    def wrap(planes):
        for i in range(PAIRS):
            for k in planes:
                bb[i, k, pl.ds(200, 8), :] = bb[i, k, pl.ds(8, 8), :]
                bb[i, k, pl.ds(0, 8), :] = bb[i, k, pl.ds(192, 8), :]

    loop(8, lambda j: products(j, 0, 4, lambda p, w, r: v[p, w, r, :], 0, lambda n, w, r: psi[n, w, r, :], 0))
    wrap((4, 5))

    loads[6].wait()
    loads[7].wait()

    def project(a):
        first = plane_s[a]
        pick = []
        for k in range(6):
            x = (2 * dom + k - 2 + 128) % 128
            pick.append([jnp.where(first + w == x, 1.0, 0.0) for w in (0, 1)])

        def block(j):
            for base, ks in ((0, (0, 1, 2, 3)), (HALF, (2, 3, 4, 5))):
                at = pl.ds(rows(j, base), BLK)
                p0, p1 = proj[a, 0, at, :], proj[a, 1, at, :]
                for k in ks:
                    pj[a, k, at, :] = pick[k][0] * p0 + pick[k][1] * p1

        loop(4, block)

    loop(ATOMS, project)

    def put(i, k, value):
        acc[pl.ds(pl.multiple_of(((PAIRS - i) % PAIRS * 16 + k) * 8, 8), 8), :] = value

    def get(i, k):
        return acc[pl.ds(pl.multiple_of(((PAIRS - i) % PAIRS * 16 + k) * 8, 8), 8), :]

    zero = jnp.zeros((8, NZ), F32)

    def own_fields(w, at):
        return [pj[a, 2 + w, at, :] for a in range(ATOMS)] + [psi[m, w, at, :] for m in range(NB)]

    def amounts(i):
        def step(j, sums):
            sums = list(sums)
            for w in (0, 1):
                for t in range(BLK // 8):
                    r = pl.multiple_of(j * BLK + 8 * t, 8)
                    x = bb[i, 4 + w, pl.ds(r + 8, 8), :]
                    for k, u in enumerate(own_fields(w, pl.ds(r, 8))):
                        sums[k] += u * x
                    sums[KU] += x * x
            return tuple(sums)

        sums = lax.fori_loop(0, 8, step, (zero,) * (KU + 1))
        for k in range(KU + 1):
            put(i, k, sums[k])

    def form_own(i):
        shift = shift_s[i % NB] + 3.75

        def step(j, total):
            for t in range(BLK // 8):
                r = pl.multiple_of(j * BLK + 8 * t, 8)
                xs = []
                for w in (0, 1):
                    x = bb[i, 4 + w, pl.ds(r + 8, 8), :]
                    s1 = bb[i, 4 + w, pl.ds(r + 9, 8), :] + pltpu.roll(x, NZ - 1, 1)
                    s2 = bb[i, 4 + w, pl.ds(r + 10, 8), :] + pltpu.roll(x, NZ - 2, 1)
                    total += x * ((lp[w, pl.ds(r, 8), :] + shift) * x - (4.0 / 3.0) * s1 + (1.0 / 12.0) * s2)
                    xs.append(x)
                total -= (4.0 / 3.0) * xs[0] * xs[1]
            return total

        return lax.fori_loop(0, 8, step, zero)

    def form_cross(i):
        def step(j, total):
            for t in range(BLK // 8):
                r = pl.multiple_of(j * BLK + 8 * t, 8)
                x2, x3, x4, x5 = [bb[i, k, pl.ds(r + 8, 8), :] for k in (2, 3, 4, 5)]
                total += x4 * ((1.0 / 12.0) * x2 - (4.0 / 3.0) * x3) + (1.0 / 12.0) * (x3 * x5)
                x4, x5, x6, x7 = [bb[i, k, pl.ds(r + 8 + HALF, 8), :] for k in (4, 5, 6, 7)]
                total += x5 * ((1.0 / 12.0) * x7 - (4.0 / 3.0) * x6) + (1.0 / 12.0) * (x4 * x6)
            return total

        return lax.fori_loop(0, 4, step, zero)

    def send_row(t):
        parts = acc[pl.ds(0, 128, stride=8), :]
        for s in range(1, 8):
            parts += acc[pl.ds(s, 128, stride=8), :]
        row = lax.dot_general(
            jnp.ones((8, NZ), F32), parts, (((1,), (1,)), ((), ())),
            precision=lax.Precision.HIGHEST, preferred_element_type=F32,
        )
        rowb[t] = row
        slots[t, pl.ds(dom, 1), :] = row[0:1]

        def one(e, _):
            xj, yj, zj = e // 16, (e // 8) % 2, e % 8
            dx = jnp.where(xj % 2 == 1, 2 - (xj + 1) // 2, 2 + xj // 2)
            dz = jnp.where(zj % 2 == 1, 4 - (zj + 1) // 2, 4 + zj // 2)
            dy = 1 - yj
            peer = ((dom // 16 + dx) % 4) * 16 + ((dom // 8 + dy) % 2) * 8 + (dom + dz) % 8
            remote(ROWS + t, rowb.at[t, pl.ds(0, 1)], slots.at[t, pl.ds(dom, 1)], (peer, pot)).start()
            return 0

        lax.fori_loop(0, DOMS - 1, one, 0)

    def rows_copy(t):
        return remote(ROWS + t, slots.at[t, pl.ds(0, DOMS - 1)], slots.at[t, pl.ds(0, DOMS - 1)], (right, pot))

    def take_row(t):
        rows_copy(t).wait_recv()
        total = jnp.sum(slots[t], axis=0, keepdims=True)
        return pltpu.roll(jnp.broadcast_to(total, (8, NZ)), 0, 1, stride=16, stride_axis=0)

    def column(m, k):
        return jnp.sum(jnp.where(lane == k, m, 0.0), axis=1, keepdims=True)

    pass_on(0, c1p)
    start(c3p)
    loop(PAIRS, amounts)
    pass_mate(0)
    loop(PAIRS, lambda i: put(i, KU + 1, form_own(i)))
    arrive(c1v)
    start(c3v)
    gathered(0)
    for s, base, planes in ((0, 0, 2), (1, HALF, 6)):
        loop(4, lambda j: products(j, base, planes, lambda p, w, r: vh1[s, p, w, r, :], 0, lambda n, w, r: ph1[s, n, w, r, :], 0))
    loop(PAIRS, lambda i: put(i, KU + 1, get(i, KU + 1) + form_cross(i)))
    pl.semaphore_wait(gate, 7)
    send_row(0)

    pass_on(1, c2p)
    pass_mate(1)
    start(vg[:2])
    arrive(c2v)
    gathered(1)
    for s, base, planes in ((0, HALF, 2), (1, 0, 6)):
        loop(4, lambda j: products(j, base, planes, lambda p, w, r: vh2[s, p, w, r, :], 0, lambda n, w, r: ph2[s, n, w, r, :], 0))
    wrap((2, 3, 6, 7))

    def local(i, k, r, lpv):
        def at(dk, dr):
            return bb[i, k + dk, pl.ds(r + 8 + dr, BLK), :]

        x = at(0, 0)
        s1 = at(-1, 0) + at(1, 0) + at(0, -1) + at(0, 1) + pltpu.roll(x, 1, 1) + pltpu.roll(x, NZ - 1, 1)
        s2 = at(-2, 0) + at(2, 0) + at(0, -2) + at(0, 2) + pltpu.roll(x, 2, 1) + pltpu.roll(x, NZ - 2, 1)
        yb[i, k - 2, pl.ds(r, BLK), :] = lpv * x - (2.0 / 3.0) * s1 + (1.0 / 24.0) * s2

    def local_own(i):
        shift = shift_s[i % NB] + 3.75

        def block(j):
            r = rows(j)
            for w in (0, 1):
                local(i, 4 + w, r, lp[w, pl.ds(r, BLK), :] + shift)

        loop(8, block)

    loop(PAIRS, local_own)

    pass_on(2, c3p)
    pass_mate(2)
    arrive(c3v)
    gathered(2)
    for s, base, planes in ((0, 0, 0), (1, HALF, 8)):
        loop(4, lambda j: products(j, base, planes, lambda p, w, r: vh3[s, p, w, r, :], 0, lambda n, w, r: ph3[s, n, w, r, :], 0))

    def local_beside(i):
        shift = shift_s[i % NB] + 3.75

        def block(j):
            for s, base, planes in ((0, 0, 2), (1, HALF, 6)):
                r = rows(j, base)
                for w in (0, 1):
                    local(i, planes + w, r, ph1[s, j, w, pl.ds(HALF, 24), :] + shift)

        loop(4, block)

    loop(PAIRS, local_beside)

    m1 = take_row(0)
    rr0 = column(m1, KU)
    alpha0 = rr0 / (column(m1, KU + 1) + jnp.sum(wvec * m1 * m1, axis=1, keepdims=True))
    coef = alpha0 * wvec * m1
    for k in range(KU):
        ct[k] = jnp.broadcast_to(column(coef, k), (8, NZ))
    ct[KU] = jnp.broadcast_to(alpha0, (8, NZ))

    def residual(i):
        scale = [ct[k, pl.ds(i, 1), :] for k in range(KU + 1)]

        def reduced(k, r, fields):
            x = bb[i, k, pl.ds(r + 8, 8), :] - scale[KU] * yb[i, k - 2, pl.ds(r, 8), :]
            y = scale[0] * fields[0]
            for c, u in zip(scale[1:KU], fields[1:]):
                y += c * u
            x = x - y
            bb[i, k, pl.ds(r + 8, 8), :] = x
            return x

        def step(j, sums):
            sums = list(sums)
            for w in (0, 1):
                for t in range(BLK // 8):
                    r = pl.multiple_of(j * BLK + 8 * t, 8)
                    fields = own_fields(w, pl.ds(r, 8))
                    x = reduced(4 + w, r, fields)
                    for k, u in enumerate(fields):
                        sums[k] += u * x
                    sums[KU] += x * x
            return tuple(sums)

        sums = lax.fori_loop(0, 8, step, (zero,) * (KU + 1))
        for k in range(KU + 1):
            put(i, k, sums[k])

        def beside(j):
            for s, base, planes in ((0, 0, 2), (1, HALF, 6)):
                for w in (0, 1):
                    for t in range(BLK // 8):
                        r0 = pl.multiple_of(j * BLK + 8 * t, 8)
                        at = pl.ds(r0 + base, 8)
                        fields = [pj[a, planes - 2 + w, at, :] for a in range(ATOMS)]
                        fields += [ph1[s, m, w, pl.ds(r0, 8), :] for m in range(NB)]
                        reduced(planes + w, r0 + base, fields)

        loop(4, beside)
        for k in (4, 5):
            bb[i, k, pl.ds(200, 8), :] = bb[i, k, pl.ds(8, 8), :]
        put(i, KU + 1, form_own(i) + form_cross(i))

    loop(PAIRS, residual)
    send_row(1)

    vg[1].wait_recv()
    vg[2].start()
    vg[0].wait_recv()
    vg[2].wait_recv()
    vall[pl.ds(2 * pot, 2)] = v[...]

    def response(i):
        p, n = i // NB, i % NB

        def step(j, sums):
            sums = list(sums)
            for w in (0, 1):
                for t in range(BLK // 8):
                    r = pl.multiple_of(j * BLK + 8 * t, 8)
                    at = pl.ds(r, 8)
                    orb = psi[n, w, at, :]
                    f0 = orb * (orb * v[p, w, at, :])
                    f1 = orb * bb[i, 4 + w, pl.ds(r + 8, 8), :]
                    for q in range(8):
                        u = vall[q, w, at, :]
                        sums[q] += u * f0
                        sums[8 + q] += u * f1
            return tuple(sums)

        sums = lax.fori_loop(0, 8, step, (zero,) * 16)
        for k in range(16):
            put(i, k, sums[k])

    loop(PAIRS, response)
    send_row(2)

    m2 = take_row(1)
    rr1 = column(m2, KU)
    curve = column(m2, KU + 1) + jnp.sum(wvec * m2 * m2, axis=1, keepdims=True)
    alpha1 = rr1 / (curve - rr1 * (rr1 / rr0) / alpha0)
    first = alpha0 + alpha1 * (rr1 / rr0)
    ct[0] = jnp.broadcast_to(-first, (8, NZ))
    ct[1] = jnp.broadcast_to(-alpha1, (8, NZ))

    def write(i):
        p, n = i // NB, i % NB
        one, two = ct[0, pl.ds(i, 1), :], ct[1, pl.ds(i, 1), :]

        def block(j):
            r = rows(j)
            for w in (0, 1):
                at = pl.ds(r, BLK)
                sol[p, n, w, at, :] = one * (v[p, w, at, :] * psi[n, w, at, :]) + two * bb[i, 4 + w, pl.ds(r + 8, BLK), :]

        loop(8, block)

    loop(PAIRS, write)
    out = pltpu.make_async_copy(sol, sol_h, lsem.at[8])
    out.start()

    m3 = take_row(2)
    each = (-2.0 / CELLS) * (first * m3 + alpha1 * pltpu.roll(m3, NZ - 8, 1))
    for p in range(LOC):
        resp_o[p : p + 1, :] = jnp.sum(each[p * NB : (p + 1) * NB, :8], axis=0, keepdims=True)

    out.wait()
    for c in c1p + c1v + c2p + c2v + c3p + c3v + list(vg):
        c.wait_send()
    for ch in spreads:
        for s in ch:
            for c in s:
                c.wait_send()
    for t in range(3):
        rows_copy(t).wait_send()


def shards(band_orbitals, local_potential, band_shift, trial_potentials, projector_blocks, atom_plane, projector_weight):
    anyspec = pl.BlockSpec(memory_space=pl.ANY)
    smem = pl.BlockSpec(memory_space=pltpu.SMEM)
    vm = lambda *shape: pltpu.VMEM(shape, F32)
    return pl.pallas_call(
        kernel,
        out_shape=(
            jax.ShapeDtypeStruct((LOC, NB, 2, NY, NZ), F32),
            jax.ShapeDtypeStruct((LOC, 8), F32),
        ),
        in_specs=[anyspec] * 4 + [smem] * 3,
        out_specs=(anyspec, pl.BlockSpec(memory_space=pltpu.VMEM)),
        scratch_shapes=[
            vm(NB, 2, NY, NZ),
            vm(LOC, 2, NY, NZ),
            vm(2, NY, NZ),
            vm(ATOMS, 2, NY, NZ),
            vm(8, 2, NY, NZ),
            vm(2, 2, HALF + 24, NZ),
            vm(2, NB, 2, HALF + 24, NZ),
            vm(2, NB, 2, HALF, NZ),
            vm(2, NB, 2, HALF, NZ),
            vm(2, LOC, 2, HALF, NZ),
            vm(2, LOC, 2, HALF, NZ),
            vm(2, LOC, 2, HALF, NZ),
            vm(PAIRS, 10, NY + 16, NZ),
            vm(PAIRS, 6, NY, NZ),
            vm(ATOMS, 6, NY, NZ),
            vm(LOC, NB, 2, NY, NZ),
            vm(1024, NZ),
            vm(KU + 1, 8, NZ),
            vm(3, 8, NZ),
            vm(3, DOMS, NZ),
            pltpu.SemaphoreType.DMA((9,)),
            pltpu.SemaphoreType.DMA((NSEM,)),
            pltpu.SemaphoreType.DMA((NSEM,)),
            pltpu.SemaphoreType.REGULAR,
        ],
        compiler_params=pltpu.CompilerParams(
            collective_id=0, has_side_effects=True, vmem_limit_bytes=48 * 2**20
        ),
    )(band_orbitals, local_potential, trial_potentials, projector_blocks, band_shift, atom_plane, projector_weight)


def solution(mesh):
    placed = (
        P(None, "dom", None, None),
        P("dom", None, None),
        P(),
        P("pot", "dom", None, None),
        P(),
        P(),
        P(),
    )
    return jax.shard_map(
        shards,
        mesh=mesh,
        in_specs=placed,
        out_specs=(P("pot", None, "dom", None, None), P("pot", None)),
        check_vma=False,
    )
```

time: 1240 us -> 107 us (0.09)
  the two profiles are of different devices: /device:TPU:8 before, /device:TPU:1 now
where the time goes in v1:
time: 107 us
  Pallas kernels  98.2 us (92%)
  local copies, waits for them, and re-layouts  8.13 us (8%)
    pallas_call x1, Pallas kernels, shards(): pl.pallas_call(kernel, out_shape=(jax.ShapeDtypeStruct((LOC, NB, 2, NY, N...  98.2 us
    unnamed x16, local copies, waits for them, and re-layouts  8.13 us

profile of v1, /device:TPU:1, one launch (start us, length us, event | category | flops | bytes accessed | tf_op | source)
XLA Modules:
  0.0 107.0 jit_solution(10098235768606308743)
XLA Ops:
  0.6 0.0 copy-start
  0.6 1.4 %copy-done = f32[8,2,192,128]{3,2,1,0:T(8,128)S(1)} copy-done((f32[8,2,192,128]{3,2,1,0:T(8,128)S(1)}, f32[8,2,192,128]{3,2,1,0:T(8,128)}, u32[]{:S(2)}) %copy-start) | copy-done | bytes 1572888
  2.0 0.0 copy-start.1
  2.0 1.1 %copy-done.1 = f32[4,2,192,128]{3,2,1,0:T(8,128)S(1)} copy-done((f32[4,2,192,128]{3,2,1,0:T(8,128)S(1)}, f32[4,2,192,128]{3,2,1,0:T(8,128)}, u32[]{:S(2)}) %copy-start.1) | copy-done | bytes 786456
  3.2 0.0 copy-start.2
  3.2 1.0 copy-done.2
  4.2 0.0 copy-start.3
  4.2 0.9 copy-done.3
  5.1 0.0 copy-start.4
  5.1 0.7 copy-done.4
  5.8 0.0 copy-start.5
  5.8 0.7 copy-done.5
  6.4 0.0 copy-start.6
  6.4 0.7 copy-done.6
  7.1 98.2 %shard_map.86 = (f32[2,4,2,192,128]{4,3,2,1,0:T(8,128)S(1)}, f32[2,8]{1,0:T(2,128)S(1)}) custom-call(f32[4,2,192,128]{3,2,1,0:T(8,128)S(1)} %copy-done.1, f32[2,192,128]{2,1,0:T(8,128)S(1)} %copy-done.3, f32[2,2,192,128]{3,2,1,0:T(8,128)S(1)} %copy-done.2, f32[8,2,192,128]{3,2,1,0:T(8,128)S(1)} %copy-done, f32[4]{0:T(128)S(1)} %copy-done.4, s32[8]{0:T(128)S(1)} %copy-done.5, ...), custom_call_target="tpu_custom_call" | custom-call | tf_op jit(solution)/shard_map/pallas_call | solution.py:472
  105.3 1.1 %copy.11 = f32[2,4,2,192,128]{4,3,2,1,0:T(8,128)} copy(f32[2,4,2,192,128]{4,3,2,1,0:T(8,128)S(1)} %get-tuple-element.4) | data formatting | bytes 3145728
  106.5 0.6 copy.12
Async XLA Ops:
  0.6 1.4 %copy-start = (f32[8,2,192,128]{3,2,1,0:T(8,128)S(1)}, f32[8,2,192,128]{3,2,1,0:T(8,128)}, u32[]{:S(2)}) copy-start(f32[8,2,192,128]{3,2,1,0:T(8,128)} %proj_h.1) | copy-start | bytes 4718596
  2.0 1.1 %copy-start.1 = (f32[4,2,192,128]{3,2,1,0:T(8,128)S(1)}, f32[4,2,192,128]{3,2,1,0:T(8,128)}, u32[]{:S(2)}) copy-start(f32[4,2,192,128]{3,2,1,0:T(8,128)} %psi_h.1) | copy-start | bytes 2359300
  3.2 1.0 copy-start.2
  4.2 0.9 copy-start.3
  5.1 0.7 copy-start.4
  5.8 0.7 copy-start.5
  6.4 0.7 copy-start.6

commit v2 on v1

--- a/solution.py
+++ b/solution.py
@@ -17,7 +17,7 @@
 BLOCK_CELLS = 2 * 192 * 128
 C1P, C1V, C2P, C2V, C3P, C3V = 0, 2, 4, 6, 8, 10
 BCAST = 12
-VG = BCAST + 18
+VG = BCAST + 6
 ROWS = VG + 3
 NSEM = ROWS + 3
 
@@ -33,11 +33,15 @@
     mate, part = (pot // 2) * 2 + 1 - pot % 2, (pot + 2) % 4
     plane_xy, zc = dom // 8, dom % 8
 
-    loads = [
-        (psi_h.at[pot, :, pl.ds(0, HALF)], stg.at[0, :, pl.ds(0, HALF)]),
-        (lp_h.at[:, pl.ds(24 * pot, 24)], stg.at[0, :, pl.ds(HALF, 24)]),
-        (psi_h.at[pot, :, pl.ds(HALF, HALF)], stg.at[1, :, pl.ds(0, HALF)]),
-        (lp_h.at[:, pl.ds(HALF + 24 * pot, 24)], stg.at[1, :, pl.ds(HALF, 24)]),
+    core = pot % 2
+    mine = pl.ds(2 * core, 2)
+    loads = []
+    for s in (0, 1):
+        loads.append((psi_h.at[mine, :, pl.ds(s * HALF, HALF)], stg.at[s, :, :, pl.ds(0, HALF)]))
+        for b in (0, 1):
+            quarter = pl.ds(s * HALF + 24 * (2 * core + b), 24)
+            loads.append((lp_h.at[:, quarter], stg.at[s, b, :, pl.ds(HALF, 24)]))
+    loads += [
         (v_h, v),
         (psi_h, psi),
         (lp_h, lp),
@@ -59,7 +63,7 @@
     for k in range(1, 8):
         greet(plane_xy * 8 + (zc + k) % 8, pot)
         greet(((plane_xy + k) % 8) * 8 + zc, pot)
-    for c in loads[:5]:
+    for c in loads[:7]:
         c.wait()
     pl.semaphore_wait(bar, 18)
 
@@ -71,22 +75,16 @@
     low, high = pl.ds(0, HALF), pl.ds(HALF, HALF)
     to = ((right, pot), (left, pot))
     near, far = (low, high), (high, low)
-    c1p = [remote(C1P + s, stg.at[s], ph1.at[s, pot], to[s]) for s in (0, 1)]
+    c1p = [remote(C1P + s, stg.at[s], ph1.at[s, mine], to[s]) for s in (0, 1)]
     c1v = [remote(C1V + s, v.at[:, :, near[s]], vh1.at[s], to[s]) for s in (0, 1)]
-    c2p = [remote(C2P + s, psi.at[pot, :, far[s]], ph2.at[s, pot], to[s]) for s in (0, 1)]
+    c2p = [remote(C2P + s, psi.at[mine, :, far[s]], ph2.at[s, mine], to[s]) for s in (0, 1)]
     c2v = [remote(C2V + s, v.at[:, :, far[s]], vh2.at[s], to[s]) for s in (0, 1)]
-    c3p = [remote(C3P + s, ph1.at[s, pot, :, low], ph3.at[s, pot], to[s]) for s in (0, 1)]
+    c3p = [remote(C3P + s, ph1.at[s, mine, :, low], ph3.at[s, mine], to[s]) for s in (0, 1)]
     c3v = [remote(C3V + s, vh1.at[s], vh3.at[s], to[s]) for s in (0, 1)]
 
     def spread(ch, s):
-        ref = (ph1, ph2, ph3)[ch]
-        i = BCAST + ch * 6 + s * 3
-        own, other = ref.at[s, pot], ref.at[s, part]
-        return (
-            remote(i, own, own, (dom, mate)),
-            remote(i + 1, own, own, (dom, part)),
-            remote(i + 2, other, other, (dom, mate)),
-        )
+        own = (ph1, ph2, ph3)[ch].at[s, mine]
+        return remote(BCAST + ch * 2 + s, own, own, (dom, mate))
 
     spreads = [[spread(ch, s) for s in (0, 1)] for ch in range(3)]
     vown, vpart = vall.at[pl.ds(2 * pot, 2)], vall.at[pl.ds(2 * part, 2)]
@@ -106,20 +104,7 @@
 
     def pass_on(ch, copies):
         arrive(copies)
-        for s in (0, 1):
-            spreads[ch][s][1].start()
-        for s in (0, 1):
-            spreads[ch][s][0].start()
-
-    def pass_mate(ch):
-        for s in (0, 1):
-            spreads[ch][s][1].wait_recv()
-            spreads[ch][s][2].start()
-
-    def gathered(ch):
-        for s in (0, 1):
-            spreads[ch][s][0].wait_recv()
-            spreads[ch][s][2].wait_recv()
+        start(spreads[ch])
 
     start(c1p)
     start(c1v)
@@ -127,7 +112,7 @@
         pl.semaphore_signal(
             gate, inc=1, device_id=(((plane_xy + k) % 8) * 8 + zc, pot), device_id_type=MESH
         )
-    loads[5].wait()
+    loads[7].wait()
     start(c2p)
     start(c2v)
 
@@ -165,8 +150,8 @@
     loop(8, lambda j: products(j, 0, 4, lambda p, w, r: v[p, w, r, :], 0, lambda n, w, r: psi[n, w, r, :], 0))
     wrap((4, 5))
 
-    loads[6].wait()
-    loads[7].wait()
+    loads[8].wait()
+    loads[9].wait()
 
     def project(a):
         first = plane_s[a]
@@ -201,47 +186,40 @@
         def step(j, sums):
             sums = list(sums)
             for w in (0, 1):
-                for t in range(BLK // 8):
-                    r = pl.multiple_of(j * BLK + 8 * t, 8)
+                for t in range(6):
+                    r = pl.multiple_of(j * 48 + 8 * t, 8)
                     x = bb[i, 4 + w, pl.ds(r + 8, 8), :]
                     for k, u in enumerate(own_fields(w, pl.ds(r, 8))):
                         sums[k] += u * x
                     sums[KU] += x * x
             return tuple(sums)
 
-        sums = lax.fori_loop(0, 8, step, (zero,) * (KU + 1))
+        sums = lax.fori_loop(0, 4, step, (zero,) * (KU + 1))
         for k in range(KU + 1):
             put(i, k, sums[k])
 
     def form_own(i):
         shift = shift_s[i % NB] + 3.75
-
-        def step(j, total):
-            for t in range(BLK // 8):
-                r = pl.multiple_of(j * BLK + 8 * t, 8)
-                xs = []
-                for w in (0, 1):
-                    x = bb[i, 4 + w, pl.ds(r + 8, 8), :]
-                    s1 = bb[i, 4 + w, pl.ds(r + 9, 8), :] + pltpu.roll(x, NZ - 1, 1)
-                    s2 = bb[i, 4 + w, pl.ds(r + 10, 8), :] + pltpu.roll(x, NZ - 2, 1)
-                    total += x * ((lp[w, pl.ds(r, 8), :] + shift) * x - (4.0 / 3.0) * s1 + (1.0 / 12.0) * s2)
-                    xs.append(x)
-                total -= (4.0 / 3.0) * xs[0] * xs[1]
-            return total
-
-        return lax.fori_loop(0, 8, step, zero)
+        total = [zero, zero]
+        for r in range(0, NY, 8):
+            xs = []
+            for w in (0, 1):
+                x = bb[i, 4 + w, pl.ds(r + 8, 8), :]
+                s1 = bb[i, 4 + w, pl.ds(r + 9, 8), :] + pltpu.roll(x, NZ - 1, 1)
+                s2 = bb[i, 4 + w, pl.ds(r + 10, 8), :] + pltpu.roll(x, NZ - 2, 1)
+                total[w] += x * ((lp[w, pl.ds(r, 8), :] + shift) * x - (4.0 / 3.0) * s1 + (1.0 / 12.0) * s2)
+                xs.append(x)
+            total[0] -= (4.0 / 3.0) * xs[0] * xs[1]
+        return total[0] + total[1]
 
     def form_cross(i):
-        def step(j, total):
-            for t in range(BLK // 8):
-                r = pl.multiple_of(j * BLK + 8 * t, 8)
-                x2, x3, x4, x5 = [bb[i, k, pl.ds(r + 8, 8), :] for k in (2, 3, 4, 5)]
-                total += x4 * ((1.0 / 12.0) * x2 - (4.0 / 3.0) * x3) + (1.0 / 12.0) * (x3 * x5)
-                x4, x5, x6, x7 = [bb[i, k, pl.ds(r + 8 + HALF, 8), :] for k in (4, 5, 6, 7)]
-                total += x5 * ((1.0 / 12.0) * x7 - (4.0 / 3.0) * x6) + (1.0 / 12.0) * (x4 * x6)
-            return total
-
-        return lax.fori_loop(0, 4, step, zero)
+        total = [zero, zero]
+        for r in range(0, HALF, 8):
+            x2, x3, x4, x5 = [bb[i, k, pl.ds(r + 8, 8), :] for k in (2, 3, 4, 5)]
+            total[0] += x4 * ((1.0 / 12.0) * x2 - (4.0 / 3.0) * x3) + (1.0 / 12.0) * (x3 * x5)
+            x4, x5, x6, x7 = [bb[i, k, pl.ds(r + 8 + HALF, 8), :] for k in (4, 5, 6, 7)]
+            total[1] += x5 * ((1.0 / 12.0) * x7 - (4.0 / 3.0) * x6) + (1.0 / 12.0) * (x4 * x6)
+        return total[0] + total[1]
 
     def send_row(t):
         parts = acc[pl.ds(0, 128, stride=8), :]
@@ -279,11 +257,10 @@
     pass_on(0, c1p)
     start(c3p)
     loop(PAIRS, amounts)
-    pass_mate(0)
     loop(PAIRS, lambda i: put(i, KU + 1, form_own(i)))
     arrive(c1v)
     start(c3v)
-    gathered(0)
+    arrive(spreads[0])
     for s, base, planes in ((0, 0, 2), (1, HALF, 6)):
         loop(4, lambda j: products(j, base, planes, lambda p, w, r: vh1[s, p, w, r, :], 0, lambda n, w, r: ph1[s, n, w, r, :], 0))
     loop(PAIRS, lambda i: put(i, KU + 1, get(i, KU + 1) + form_cross(i)))
@@ -291,56 +268,47 @@
     send_row(0)
 
     pass_on(1, c2p)
-    pass_mate(1)
-    start(vg[:2])
     arrive(c2v)
-    gathered(1)
+    arrive(spreads[1])
     for s, base, planes in ((0, HALF, 2), (1, 0, 6)):
         loop(4, lambda j: products(j, base, planes, lambda p, w, r: vh2[s, p, w, r, :], 0, lambda n, w, r: ph2[s, n, w, r, :], 0))
     wrap((2, 3, 6, 7))
 
     def local(i, k, r, lpv):
         def at(dk, dr):
-            return bb[i, k + dk, pl.ds(r + 8 + dr, BLK), :]
+            return bb[i, k + dk, pl.ds(r + 8 + dr, 8), :]
 
         x = at(0, 0)
         s1 = at(-1, 0) + at(1, 0) + at(0, -1) + at(0, 1) + pltpu.roll(x, 1, 1) + pltpu.roll(x, NZ - 1, 1)
         s2 = at(-2, 0) + at(2, 0) + at(0, -2) + at(0, 2) + pltpu.roll(x, 2, 1) + pltpu.roll(x, NZ - 2, 1)
-        yb[i, k - 2, pl.ds(r, BLK), :] = lpv * x - (2.0 / 3.0) * s1 + (1.0 / 24.0) * s2
+        yb[i, k - 2, pl.ds(r, 8), :] = lpv * x - (2.0 / 3.0) * s1 + (1.0 / 24.0) * s2
 
     def local_own(i):
         shift = shift_s[i % NB] + 3.75
-
-        def block(j):
-            r = rows(j)
-            for w in (0, 1):
-                local(i, 4 + w, r, lp[w, pl.ds(r, BLK), :] + shift)
-
-        loop(8, block)
+        for r in range(0, NY, 8):
+            for w in (0, 1):
+                local(i, 4 + w, r, lp[w, pl.ds(r, 8), :] + shift)
 
     loop(PAIRS, local_own)
 
     pass_on(2, c3p)
-    pass_mate(2)
     arrive(c3v)
-    gathered(2)
+    arrive(spreads[2])
     for s, base, planes in ((0, 0, 0), (1, HALF, 8)):
         loop(4, lambda j: products(j, base, planes, lambda p, w, r: vh3[s, p, w, r, :], 0, lambda n, w, r: ph3[s, n, w, r, :], 0))
 
     def local_beside(i):
         shift = shift_s[i % NB] + 3.75
-
-        def block(j):
+        for r in range(0, HALF, 8):
             for s, base, planes in ((0, 0, 2), (1, HALF, 6)):
-                r = rows(j, base)
                 for w in (0, 1):
-                    local(i, planes + w, r, ph1[s, j, w, pl.ds(HALF, 24), :] + shift)
-
-        loop(4, block)
+                    lpv = ph1[s, r // 24, w, pl.ds(HALF + r % 24, 8), :]
+                    local(i, planes + w, base + r, lpv + shift)
 
     loop(PAIRS, local_beside)
 
     m1 = take_row(0)
+    start(vg[:2])
     rr0 = column(m1, KU)
     alpha0 = rr0 / (column(m1, KU + 1) + jnp.sum(wvec * m1 * m1, axis=1, keepdims=True))
     coef = alpha0 * wvec * m1
@@ -363,8 +331,8 @@
         def step(j, sums):
             sums = list(sums)
             for w in (0, 1):
-                for t in range(BLK // 8):
-                    r = pl.multiple_of(j * BLK + 8 * t, 8)
+                for t in range(6):
+                    r = pl.multiple_of(j * 48 + 8 * t, 8)
                     fields = own_fields(w, pl.ds(r, 8))
                     x = reduced(4 + w, r, fields)
                     for k, u in enumerate(fields):
@@ -372,21 +340,21 @@
                     sums[KU] += x * x
             return tuple(sums)
 
-        sums = lax.fori_loop(0, 8, step, (zero,) * (KU + 1))
+        sums = lax.fori_loop(0, 4, step, (zero,) * (KU + 1))
         for k in range(KU + 1):
             put(i, k, sums[k])
 
         def beside(j):
             for s, base, planes in ((0, 0, 2), (1, HALF, 6)):
                 for w in (0, 1):
-                    for t in range(BLK // 8):
-                        r0 = pl.multiple_of(j * BLK + 8 * t, 8)
+                    for t in range(6):
+                        r0 = pl.multiple_of(j * 48 + 8 * t, 8)
                         at = pl.ds(r0 + base, 8)
                         fields = [pj[a, planes - 2 + w, at, :] for a in range(ATOMS)]
                         fields += [ph1[s, m, w, pl.ds(r0, 8), :] for m in range(NB)]
                         reduced(planes + w, r0 + base, fields)
 
-        loop(4, beside)
+        loop(2, beside)
         for k in (4, 5):
             bb[i, k, pl.ds(200, 8), :] = bb[i, k, pl.ds(8, 8), :]
         put(i, KU + 1, form_own(i) + form_cross(i))
@@ -406,8 +374,8 @@
         def step(j, sums):
             sums = list(sums)
             for w in (0, 1):
-                for t in range(BLK // 8):
-                    r = pl.multiple_of(j * BLK + 8 * t, 8)
+                for t in range(6):
+                    r = pl.multiple_of(j * 48 + 8 * t, 8)
                     at = pl.ds(r, 8)
                     orb = psi[n, w, at, :]
                     f0 = orb * (orb * v[p, w, at, :])
@@ -418,7 +386,7 @@
                         sums[8 + q] += u * f1
             return tuple(sums)
 
-        sums = lax.fori_loop(0, 8, step, (zero,) * 16)
+        sums = lax.fori_loop(0, 4, step, (zero,) * 16)
         for k in range(16):
             put(i, k, sums[k])
 
@@ -446,7 +414,7 @@
         loop(8, block)
 
     loop(PAIRS, write)
-    out = pltpu.make_async_copy(sol, sol_h, lsem.at[8])
+    out = pltpu.make_async_copy(sol, sol_h, lsem.at[10])
     out.start()
 
     m3 = take_row(2)
@@ -459,14 +427,13 @@
         c.wait_send()
     for ch in spreads:
         for s in ch:
-            for c in s:
-                c.wait_send()
+            s.wait_send()
     for t in range(3):
         rows_copy(t).wait_send()
 
 
 def shards(band_orbitals, local_potential, band_shift, trial_potentials, projector_blocks, atom_plane, projector_weight):
-    anyspec = pl.BlockSpec(memory_space=pl.ANY)
+    anyspec = pl.BlockSpec(memory_space=pltpu.HBM)
     smem = pl.BlockSpec(memory_space=pltpu.SMEM)
     vm = lambda *shape: pltpu.VMEM(shape, F32)
     return pl.pallas_call(
@@ -483,7 +450,7 @@
             vm(2, NY, NZ),
             vm(ATOMS, 2, NY, NZ),
             vm(8, 2, NY, NZ),
-            vm(2, 2, HALF + 24, NZ),
+            vm(2, 2, 2, HALF + 24, NZ),
             vm(2, NB, 2, HALF + 24, NZ),
             vm(2, NB, 2, HALF, NZ),
             vm(2, NB, 2, HALF, NZ),
@@ -498,13 +465,13 @@
             vm(KU + 1, 8, NZ),
             vm(3, 8, NZ),
             vm(3, DOMS, NZ),
-            pltpu.SemaphoreType.DMA((9,)),
+            pltpu.SemaphoreType.DMA((11,)),
             pltpu.SemaphoreType.DMA((NSEM,)),
             pltpu.SemaphoreType.DMA((NSEM,)),
             pltpu.SemaphoreType.REGULAR,
         ],
         compiler_params=pltpu.CompilerParams(
-            collective_id=0, has_side_effects=True, vmem_limit_bytes=48 * 2**20
+            collective_id=0, has_side_effects=True, vmem_limit_bytes=63 * 2**20
         ),
     )(band_orbitals, local_potential, trial_potentials, projector_blocks, band_shift, atom_plane, projector_weight)
 

time: 107 us -> 71.1 us (0.66)
  Pallas kernels: 98.2 us -> 67.1 us
  local copies, waits for them, and re-layouts: 8.13 us -> 3.27 us
    pallas_call x1, Pallas kernels: 98.2 us -> 67.1 us  [shards(): pl.pallas_call(kernel, out_shape=(jax.ShapeDtypeStruct((LOC, NB, 2, NY, N...]
    unnamed x16 -> x4, local copies, waits for them, and re-layouts: 8.13 us -> 3.27 us
where the time goes in v2:
time: 71.1 us; the launch traced here: 71 us
  Pallas kernels  67.1 us (94%)
  local copies, waits for them, and re-layouts  3.27 us (5%)
    pallas_call x1, Pallas kernels, shards(): pl.pallas_call(kernel, out_shape=(jax.ShapeDtypeStruct((LOC, NB, 2, NY, N...  67.1 us
    unnamed x4, local copies, waits for them, and re-layouts  3.27 us

profile of v2, /device:TPU:1, one launch (start us, length us, event | category | flops | bytes accessed | tf_op | source)
XLA Modules:
  0.0 71.0 jit_solution(13071978068649029082)
XLA Ops:
  0.6 67.1 %shard_map.86 = (f32[2,4,2,192,128]{4,3,2,1,0:T(8,128)}, f32[2,8]{1,0:T(2,128)}) custom-call(f32[4,2,192,128]{3,2,1,0:T(8,128)} %psi_h.1, f32[2,192,128]{2,1,0:T(8,128)} %lp_h.1, f32[2,2,192,128]{3,2,1,0:T(8,128)} %v_h.1, f32[8,2,192,128]{3,2,1,0:T(8,128)} %proj_h.1, f32[4]{0:T(128)} %shift_s.1, s32[8]{0:T(128)} %plane_s.1, f32[8]{0:T(128)} %weight_s.1), custom_call_target="tpu_custom_call" | custom-call | tf_op jit(solution)/shard_map/pallas_call | solution.py:439
  67.7 0.0 copy-start
  67.8 2.7 %copy.11 = f32[2,4,2,192,128]{4,3,2,1,0:T(8,128)} copy(f32[2,4,2,192,128]{4,3,2,1,0:T(8,128)} %get-tuple-element.4) | data formatting | bytes 3145728
  70.5 0.0 copy-done
  70.5 0.6 copy.12
Async XLA Ops:
  67.7 2.7 %copy-start = (f32[2,8]{1,0:T(2,128)S(1)}, f32[2,8]{1,0:T(2,128)}, u32[]{:S(2)}) copy-start(f32[2,8]{1,0:T(2,128)} %get-tuple-element.5) | copy-start | bytes 196

commit v3 on v2

--- a/solution.py
+++ b/solution.py
@@ -26,12 +26,13 @@
     psi_h, lp_h, v_h, proj_h, shift_s, plane_s, weight_s,
     sol_h, resp_o,
     psi, v, lp, proj, vall, stg, ph1, ph2, ph3, vh1, vh2, vh3,
-    bb, yb, pj, sol, acc, ct, rowb, slots, lsem, ss, rs, gate,
+    bb, rb, yb, pj, sol, acc, racc, ct, rowb, slots, lsem, ss, rs, gate,
 ):
     dom, pot = lax.axis_index("dom"), lax.axis_index("pot")
     right, left = (dom + 1) % DOMS, (dom + DOMS - 1) % DOMS
     mate, part = (pot // 2) * 2 + 1 - pot % 2, (pot + 2) % 4
     plane_xy, zc = dom // 8, dom % 8
+    ring = [lax.rem(zc + d, 8) for d in (4, 3, 5, 2, 6, 1, 7, 0)]
 
     core = pot % 2
     mine = pl.ds(2 * core, 2)
@@ -171,8 +172,8 @@
 
     loop(ATOMS, project)
 
-    def put(i, k, value):
-        acc[pl.ds(pl.multiple_of(((PAIRS - i) % PAIRS * 16 + k) * 8, 8), 8), :] = value
+    def put(i, k, value, ref=acc):
+        ref[pl.ds(pl.multiple_of(((PAIRS - i) % PAIRS * 16 + k) * 8, 8), 8), :] = value
 
     def get(i, k):
         return acc[pl.ds(pl.multiple_of(((PAIRS - i) % PAIRS * 16 + k) * 8, 8), 8), :]
@@ -198,33 +199,35 @@
         for k in range(KU + 1):
             put(i, k, sums[k])
 
-    def form_own(i):
+    def form_own(i, ref, first):
         shift = shift_s[i % NB] + 3.75
         total = [zero, zero]
         for r in range(0, NY, 8):
             xs = []
             for w in (0, 1):
-                x = bb[i, 4 + w, pl.ds(r + 8, 8), :]
-                s1 = bb[i, 4 + w, pl.ds(r + 9, 8), :] + pltpu.roll(x, NZ - 1, 1)
-                s2 = bb[i, 4 + w, pl.ds(r + 10, 8), :] + pltpu.roll(x, NZ - 2, 1)
+                x = ref[i, first + w, pl.ds(r + 8, 8), :]
+                s1 = ref[i, first + w, pl.ds(r + 9, 8), :] + pltpu.roll(x, NZ - 1, 1)
+                s2 = ref[i, first + w, pl.ds(r + 10, 8), :] + pltpu.roll(x, NZ - 2, 1)
                 total[w] += x * ((lp[w, pl.ds(r, 8), :] + shift) * x - (4.0 / 3.0) * s1 + (1.0 / 12.0) * s2)
                 xs.append(x)
             total[0] -= (4.0 / 3.0) * xs[0] * xs[1]
         return total[0] + total[1]
 
-    def form_cross(i):
+    def form_cross(i, ref, first):
         total = [zero, zero]
         for r in range(0, HALF, 8):
-            x2, x3, x4, x5 = [bb[i, k, pl.ds(r + 8, 8), :] for k in (2, 3, 4, 5)]
+            x2, x3 = [bb[i, k, pl.ds(r + 8, 8), :] for k in (2, 3)]
+            x4, x5 = [ref[i, first + w, pl.ds(r + 8, 8), :] for w in (0, 1)]
             total[0] += x4 * ((1.0 / 12.0) * x2 - (4.0 / 3.0) * x3) + (1.0 / 12.0) * (x3 * x5)
-            x4, x5, x6, x7 = [bb[i, k, pl.ds(r + 8 + HALF, 8), :] for k in (4, 5, 6, 7)]
+            x4, x5 = [ref[i, first + w, pl.ds(r + 8 + HALF, 8), :] for w in (0, 1)]
+            x6, x7 = [bb[i, k, pl.ds(r + 8 + HALF, 8), :] for k in (6, 7)]
             total[1] += x5 * ((1.0 / 12.0) * x7 - (4.0 / 3.0) * x6) + (1.0 / 12.0) * (x4 * x6)
         return total[0] + total[1]
 
-    def send_row(t):
-        parts = acc[pl.ds(0, 128, stride=8), :]
+    def send_row(t, ref):
+        parts = ref[pl.ds(0, 128, stride=8), :]
         for s in range(1, 8):
-            parts += acc[pl.ds(s, 128, stride=8), :]
+            parts += ref[pl.ds(s, 128, stride=8), :]
         row = lax.dot_general(
             jnp.ones((8, NZ), F32), parts, (((1,), (1,)), ((), ())),
             precision=lax.Precision.HIGHEST, preferred_element_type=F32,
@@ -232,16 +235,19 @@
         rowb[t] = row
         slots[t, pl.ds(dom, 1), :] = row[0:1]
 
-        def one(e, _):
-            xj, yj, zj = e // 16, (e // 8) % 2, e % 8
-            dx = jnp.where(xj % 2 == 1, 2 - (xj + 1) // 2, 2 + xj // 2)
-            dz = jnp.where(zj % 2 == 1, 4 - (zj + 1) // 2, 4 + zj // 2)
-            dy = 1 - yj
-            peer = ((dom // 16 + dx) % 4) * 16 + ((dom // 8 + dy) % 2) * 8 + (dom + dz) % 8
-            remote(ROWS + t, rowb.at[t, pl.ds(0, 1)], slots.at[t, pl.ds(dom, 1)], (peer, pot)).start()
+        def give(xy, places):
+            for z in places:
+                remote(ROWS + t, rowb.at[t, pl.ds(0, 1)], slots.at[t, pl.ds(dom, 1)], (xy * 8 + z, pot)).start()
+
+        def plane(e, _):
+            xj, yj = lax.div(e, 2), lax.rem(e, 2)
+            dx = jnp.where(xj == 0, 2, jnp.where(xj == 1, 1, 3 - 3 * (xj - 2)))
+            x = lax.rem(lax.div(plane_xy, 2) + dx, 4)
+            give(x * 2 + lax.rem(plane_xy + 1 - yj, 2), ring)
             return 0
 
-        lax.fori_loop(0, DOMS - 1, one, 0)
+        lax.fori_loop(0, 7, plane, 0)
+        give(plane_xy, ring[:7])
 
     def rows_copy(t):
         return remote(ROWS + t, slots.at[t, pl.ds(0, DOMS - 1)], slots.at[t, pl.ds(0, DOMS - 1)], (right, pot))
@@ -255,19 +261,20 @@
         return jnp.sum(jnp.where(lane == k, m, 0.0), axis=1, keepdims=True)
 
     pass_on(0, c1p)
-    start(c3p)
     loop(PAIRS, amounts)
-    loop(PAIRS, lambda i: put(i, KU + 1, form_own(i)))
+    loop(PAIRS, lambda i: put(i, KU + 1, form_own(i, bb, 4)))
     arrive(c1v)
-    start(c3v)
     arrive(spreads[0])
     for s, base, planes in ((0, 0, 2), (1, HALF, 6)):
         loop(4, lambda j: products(j, base, planes, lambda p, w, r: vh1[s, p, w, r, :], 0, lambda n, w, r: ph1[s, n, w, r, :], 0))
-    loop(PAIRS, lambda i: put(i, KU + 1, get(i, KU + 1) + form_cross(i)))
+    loop(PAIRS, lambda i: put(i, KU + 1, get(i, KU + 1) + form_cross(i, bb, 4)))
     pl.semaphore_wait(gate, 7)
-    send_row(0)
+    send_row(0, acc)
 
     pass_on(1, c2p)
+    start(vg[:2])
+    start(c3p)
+    start(c3v)
     arrive(c2v)
     arrive(spreads[1])
     for s, base, planes in ((0, HALF, 2), (1, 0, 6)):
@@ -290,6 +297,53 @@
                 local(i, 4 + w, r, lp[w, pl.ds(r, 8), :] + shift)
 
     loop(PAIRS, local_own)
+
+    m1 = take_row(0)
+    rr0 = column(m1, KU)
+    alpha0 = rr0 / (column(m1, KU + 1) + jnp.sum(wvec * m1 * m1, axis=1, keepdims=True))
+    coef = alpha0 * wvec * m1
+    for k in range(KU):
+        ct[k] = jnp.broadcast_to(column(coef, k), (8, NZ))
+    ct[KU] = jnp.broadcast_to(alpha0, (8, NZ))
+
+    def reducer(i):
+        scale = [ct[k, pl.ds(i, 1), :] for k in range(KU + 1)]
+
+        def reduced(k, r, fields, ref, place):
+            x = bb[i, k, pl.ds(r + 8, 8), :] - scale[KU] * yb[i, k - 2, pl.ds(r, 8), :]
+            y = scale[0] * fields[0]
+            for c, u in zip(scale[1:KU], fields[1:]):
+                y += c * u
+            x = x - y
+            ref[i, place, pl.ds(r + 8, 8), :] = x
+            return x
+
+        return reduced
+
+    def residual_own(i):
+        reduced = reducer(i)
+
+        def step(j, sums):
+            sums = list(sums)
+            for w in (0, 1):
+                for t in range(6):
+                    r = pl.multiple_of(j * 48 + 8 * t, 8)
+                    fields = own_fields(w, pl.ds(r, 8))
+                    x = reduced(4 + w, r, fields, rb, w)
+                    for k, u in enumerate(fields):
+                        sums[k] += u * x
+                    sums[KU] += x * x
+            return tuple(sums)
+
+        sums = lax.fori_loop(0, 4, step, (zero,) * (KU + 1))
+        for k in range(KU + 1):
+            put(i, k, sums[k])
+
+        for w in (0, 1):
+            rb[i, w, pl.ds(200, 8), :] = rb[i, w, pl.ds(8, 8), :]
+        put(i, KU + 1, form_own(i, rb, 0))
+
+    loop(PAIRS, residual_own)
 
     pass_on(2, c3p)
     arrive(c3v)
@@ -307,42 +361,8 @@
 
     loop(PAIRS, local_beside)
 
-    m1 = take_row(0)
-    start(vg[:2])
-    rr0 = column(m1, KU)
-    alpha0 = rr0 / (column(m1, KU + 1) + jnp.sum(wvec * m1 * m1, axis=1, keepdims=True))
-    coef = alpha0 * wvec * m1
-    for k in range(KU):
-        ct[k] = jnp.broadcast_to(column(coef, k), (8, NZ))
-    ct[KU] = jnp.broadcast_to(alpha0, (8, NZ))
-
-    def residual(i):
-        scale = [ct[k, pl.ds(i, 1), :] for k in range(KU + 1)]
-
-        def reduced(k, r, fields):
-            x = bb[i, k, pl.ds(r + 8, 8), :] - scale[KU] * yb[i, k - 2, pl.ds(r, 8), :]
-            y = scale[0] * fields[0]
-            for c, u in zip(scale[1:KU], fields[1:]):
-                y += c * u
-            x = x - y
-            bb[i, k, pl.ds(r + 8, 8), :] = x
-            return x
-
-        def step(j, sums):
-            sums = list(sums)
-            for w in (0, 1):
-                for t in range(6):
-                    r = pl.multiple_of(j * 48 + 8 * t, 8)
-                    fields = own_fields(w, pl.ds(r, 8))
-                    x = reduced(4 + w, r, fields)
-                    for k, u in enumerate(fields):
-                        sums[k] += u * x
-                    sums[KU] += x * x
-            return tuple(sums)
-
-        sums = lax.fori_loop(0, 4, step, (zero,) * (KU + 1))
-        for k in range(KU + 1):
-            put(i, k, sums[k])
+    def residual_beside(i):
+        reduced = reducer(i)
 
         def beside(j):
             for s, base, planes in ((0, 0, 2), (1, HALF, 6)):
@@ -352,15 +372,13 @@
                         at = pl.ds(r0 + base, 8)
                         fields = [pj[a, planes - 2 + w, at, :] for a in range(ATOMS)]
                         fields += [ph1[s, m, w, pl.ds(r0, 8), :] for m in range(NB)]
-                        reduced(planes + w, r0 + base, fields)
+                        reduced(planes + w, r0 + base, fields, bb, planes + w)
 
         loop(2, beside)
-        for k in (4, 5):
-            bb[i, k, pl.ds(200, 8), :] = bb[i, k, pl.ds(8, 8), :]
-        put(i, KU + 1, form_own(i) + form_cross(i))
-
-    loop(PAIRS, residual)
-    send_row(1)
+        put(i, KU + 1, get(i, KU + 1) + form_cross(i, rb, 0))
+
+    loop(PAIRS, residual_beside)
+    send_row(1, acc)
 
     vg[1].wait_recv()
     vg[2].start()
@@ -378,8 +396,8 @@
                     r = pl.multiple_of(j * 48 + 8 * t, 8)
                     at = pl.ds(r, 8)
                     orb = psi[n, w, at, :]
-                    f0 = orb * (orb * v[p, w, at, :])
-                    f1 = orb * bb[i, 4 + w, pl.ds(r + 8, 8), :]
+                    f0 = orb * bb[i, 4 + w, pl.ds(r + 8, 8), :]
+                    f1 = orb * rb[i, w, pl.ds(r + 8, 8), :]
                     for q in range(8):
                         u = vall[q, w, at, :]
                         sums[q] += u * f0
@@ -388,10 +406,10 @@
 
         sums = lax.fori_loop(0, 4, step, (zero,) * 16)
         for k in range(16):
-            put(i, k, sums[k])
+            put(i, k, sums[k], racc)
 
     loop(PAIRS, response)
-    send_row(2)
+    send_row(2, racc)
 
     m2 = take_row(1)
     rr1 = column(m2, KU)
@@ -409,7 +427,7 @@
             r = rows(j)
             for w in (0, 1):
                 at = pl.ds(r, BLK)
-                sol[p, n, w, at, :] = one * (v[p, w, at, :] * psi[n, w, at, :]) + two * bb[i, 4 + w, pl.ds(r + 8, BLK), :]
+                sol[p, n, w, at, :] = one * bb[i, 4 + w, pl.ds(r + 8, BLK), :] + two * rb[i, w, pl.ds(r + 8, BLK), :]
 
         loop(8, block)
 
@@ -458,9 +476,11 @@
             vm(2, LOC, 2, HALF, NZ),
             vm(2, LOC, 2, HALF, NZ),
             vm(PAIRS, 10, NY + 16, NZ),
+            vm(PAIRS, 2, NY + 16, NZ),
             vm(PAIRS, 6, NY, NZ),
             vm(ATOMS, 6, NY, NZ),
             vm(LOC, NB, 2, NY, NZ),
+            vm(1024, NZ),
             vm(1024, NZ),
             vm(KU + 1, 8, NZ),
             vm(3, 8, NZ),

time: 71.1 us -> 64 us (0.900)
  Pallas kernels: 67.1 us -> 60 us
    pallas_call x1, Pallas kernels: 67.1 us -> 60 us  [shards(): pl.pallas_call(kernel, out_shape=(jax.ShapeDtypeStruct((LOC, NB, 2, NY, N...]
where the time goes in v3:
time: 64 us; the launch traced here: 63.9 us
  Pallas kernels  60 us (94%)
  local copies, waits for them, and re-layouts  3.27 us (5%)
  between operations  0.65 us (1%)
    pallas_call x1, Pallas kernels, shards(): pl.pallas_call(kernel, out_shape=(jax.ShapeDtypeStruct((LOC, NB, 2, NY, N...  60 us
    unnamed x4, local copies, waits for them, and re-layouts  3.27 us

profile of v3, /device:TPU:1, one launch (start us, length us, event | category | flops | bytes accessed | tf_op | source)
XLA Modules:
  0.0 63.9 jit_solution(12963793510820934575)
XLA Ops:
  0.6 60.0 %shard_map.86 = (f32[2,4,2,192,128]{4,3,2,1,0:T(8,128)}, f32[2,8]{1,0:T(2,128)}) custom-call(f32[4,2,192,128]{3,2,1,0:T(8,128)} %psi_h.1, f32[2,192,128]{2,1,0:T(8,128)} %lp_h.1, f32[2,2,192,128]{3,2,1,0:T(8,128)} %v_h.1, f32[8,2,192,128]{3,2,1,0:T(8,128)} %proj_h.1, f32[4]{0:T(128)} %shift_s.1, s32[8]{0:T(128)} %plane_s.1, f32[8]{0:T(128)} %weight_s.1), custom_call_target="tpu_custom_call" | custom-call | tf_op jit(solution)/shard_map/pallas_call | solution.py:457
  60.6 0.0 copy-start
  60.6 2.7 %copy.11 = f32[2,4,2,192,128]{4,3,2,1,0:T(8,128)} copy(f32[2,4,2,192,128]{4,3,2,1,0:T(8,128)} %get-tuple-element.4) | data formatting | bytes 3145728
  63.3 0.0 copy-done
  63.3 0.6 copy.12
Async XLA Ops:
  60.6 2.7 %copy-start = (f32[2,8]{1,0:T(2,128)S(1)}, f32[2,8]{1,0:T(2,128)}, u32[]{:S(2)}) copy-start(f32[2,8]{1,0:T(2,128)} %get-tuple-element.5) | copy-start | bytes 196

commit v4 on v3

--- a/solution.py
+++ b/solution.py
@@ -480,8 +480,8 @@
             vm(PAIRS, 6, NY, NZ),
             vm(ATOMS, 6, NY, NZ),
             vm(LOC, NB, 2, NY, NZ),
-            vm(1024, NZ),
-            vm(1024, NZ),
+            vm(1032, NZ),
+            vm(1032, NZ),
             vm(KU + 1, 8, NZ),
             vm(3, 8, NZ),
             vm(3, DOMS, NZ),

time: 64 us -> 64 us (level)
  no operation moved by 1% of the time
where the time goes in v4:
time: 64 us; the launch traced here: 63.9 us
  Pallas kernels  60 us (94%)
  local copies, waits for them, and re-layouts  3.27 us (5%)
  between operations  0.65 us (1%)
    pallas_call x1, Pallas kernels, shards(): pl.pallas_call(kernel, out_shape=(jax.ShapeDtypeStruct((LOC, NB, 2, NY, N...  60 us
    unnamed x4, local copies, waits for them, and re-layouts  3.27 us

profile of v4, /device:TPU:1, one launch (start us, length us, event | category | flops | bytes accessed | tf_op | source)
XLA Modules:
  0.0 63.9 jit_solution(552468832839686464)
XLA Ops:
  0.6 60.0 %shard_map.86 = (f32[2,4,2,192,128]{4,3,2,1,0:T(8,128)}, f32[2,8]{1,0:T(2,128)}) custom-call(f32[4,2,192,128]{3,2,1,0:T(8,128)} %psi_h.1, f32[2,192,128]{2,1,0:T(8,128)} %lp_h.1, f32[2,2,192,128]{3,2,1,0:T(8,128)} %v_h.1, f32[8,2,192,128]{3,2,1,0:T(8,128)} %proj_h.1, f32[4]{0:T(128)} %shift_s.1, s32[8]{0:T(128)} %plane_s.1, f32[8]{0:T(128)} %weight_s.1), custom_call_target="tpu_custom_call" | custom-call | tf_op jit(solution)/shard_map/pallas_call | solution.py:457
  60.6 0.0 copy-start
  60.6 2.7 %copy.11 = f32[2,4,2,192,128]{4,3,2,1,0:T(8,128)} copy(f32[2,4,2,192,128]{4,3,2,1,0:T(8,128)} %get-tuple-element.4) | data formatting | bytes 3145728
  63.3 0.0 copy-done
  63.3 0.6 copy.12
Async XLA Ops:
  60.6 2.7 %copy-start = (f32[2,8]{1,0:T(2,128)S(1)}, f32[2,8]{1,0:T(2,128)}, u32[]{:S(2)}) copy-start(f32[2,8]{1,0:T(2,128)} %get-tuple-element.5) | copy-start | bytes 196
